TPU v7x, 32 devices: a whole 2x2x4 slice. The times are simulated.
32 devices in a mesh: param: 8 (over z, x), ex: 4 (over y, core).
Axes of the slice: x: 2, y: 2, z: 4, core: 2. Of those that a mesh axis runs over, the one named last changes fastest.
Arguments:
- gradients: bfloat16 [512, 65536], P('ex', 'param'), may hold values from -60 to 60
- projection_seed: int32 [1], replicated, may hold values from 0 to 1048575
- target_features: bfloat16 [512, 4096], replicated, may hold values from -0.09375 to 0.09375
Outputs:
- scores: float32 [512, 512], P('param', 'ex')
All inputs are finite; a program needn't handle non-finite values.
Results may differ from a plain program's by a relative error of at most 0.011.
Values may be sent and summed in bfloat16 or wider, within the bound.
A program may use at most 64 MiB of HBM per device.

v0:
```python
import math

import jax
import jax.numpy as jnp
from jax import lax
from jax.sharding import PartitionSpec as P

FEATS = 4096
BLOCK = 128
STEPS = 10


DAMPING = 0.001


def partner_2(array, axis, distance):
    return lax.ppermute(array, axis, [(i, i ^ 1 << distance) for i in range(lax.axis_size(axis))])


def hashed(seed_value, row_start, row_count, col_start, col_count, total_coords):
    row_index = (row_start + lax.iota(jnp.int32, row_count)).reshape(row_count, 1)
    col_index = (col_start + lax.iota(jnp.int32, col_count)).reshape(1, col_count)
    mixed = row_index * 73856093 ^ col_index * 19349663 ^ seed_value * 83492791
    mixed = mixed ^ jnp.right_shift(mixed, 13)
    mixed = mixed * 1274126177
    mixed = mixed ^ jnp.right_shift(mixed, 16)
    uniform_value = (mixed & 65535).astype(jnp.float32) * (1.0 / 65536.0)
    return ((2.0 * uniform_value - 1.0) * math.sqrt(3.0 / total_coords)).astype(jnp.bfloat16)


def newton_inverse(fisher):
    width = fisher.shape[1]
    identity = jnp.eye(width, dtype=jnp.float32)
    trace_value = jnp.einsum("bii->b", fisher)
    damped = fisher + (DAMPING * trace_value)[:, None, None] * identity
    total = jnp.einsum("bii->b", damped)
    iterate = identity[None] / total[:, None, None]
    for _ in range(STEPS):
        product = jnp.einsum("bij,bjk->bik", damped, iterate, precision=lax.Precision.HIGHEST)
        iterate = jnp.einsum(
            "bij,bjk->bik", iterate, 2.0 * identity - product, precision=lax.Precision.HIGHEST
        )
    return iterate


def to_targets(partial_scores):
    return lax.all_to_all(partial_scores, "param", split_axis=0, concat_axis=1, tiled=True)


def on_device(gradients, projection_seed, target_features):
    seed_value = projection_seed[0]
    my_index = lax.axis_index("param")
    param_count = lax.axis_size("param")
    exam_dev, coord_dev = gradients.shape
    total_coords = coord_dev * param_count
    row_start = my_index * coord_dev
    examples_total = exam_dev * lax.axis_size("ex")
    feats_owned = FEATS // param_count
    piece_width = math.gcd(feats_owned * lax.axis_size("param"), 512)

    def project_piece(col_start):
        matrix = hashed(seed_value, row_start, coord_dev, col_start, piece_width, total_coords)
        return jnp.dot(gradients, matrix, preferred_element_type=jnp.float32).T

    starts = piece_width * lax.iota(jnp.int32, feats_owned * lax.axis_size("param") // piece_width)
    pieces = lax.map(project_piece, starts)
    owned = lax.psum_scatter(
        pieces.reshape(feats_owned * lax.axis_size("param"), exam_dev),
        "param",
        scatter_dimension=0,
        tiled=True,
    ).astype(jnp.bfloat16)
    if feats_owned < BLOCK:
        partner = partner_2(owned, "param", 0)
        is_lower = my_index % 2 == 0
        block_rows = jnp.concatenate(
            [jnp.where(is_lower, owned, partner), jnp.where(is_lower, partner, owned)], 0
        )
    else:
        block_rows = owned
    block_total = block_rows.shape[0] // BLOCK
    blocks = block_rows.reshape(block_total, BLOCK, exam_dev)
    partial_fisher = jnp.einsum("bie,bje->bij", blocks, blocks, preferred_element_type=jnp.float32)
    fisher = lax.psum(partial_fisher, "ex") / examples_total
    inverse_bf = newton_inverse(fisher).astype(jnp.bfloat16)
    conditioned = jnp.einsum("bmj,bme->bje", inverse_bf, blocks, preferred_element_type=jnp.float32)
    conditioned = conditioned.astype(jnp.bfloat16).reshape(block_rows.shape[0], exam_dev)
    if feats_owned < BLOCK:
        conditioned = lax.dynamic_slice_in_dim(
            conditioned, my_index % 2 * feats_owned, feats_owned, 0
        )
    example_rows = lax.all_to_all(conditioned, "param", split_axis=1, concat_axis=0, tiled=True)
    return to_targets(jnp.dot(target_features, example_rows, preferred_element_type=jnp.float32))


def solution(mesh):
    placed = (P("ex", "param"), P(), P())
    return jax.shard_map(
        on_device, mesh=mesh, in_specs=placed, out_specs=P("param", "ex"), check_vma=False
    )
```

profile of v0, /device:TPU:0, one launch (start us, length us, event | category | flops | bytes accessed | tf_op | source)
XLA Modules:
  0.0 246.0 jit_solution(8925204844540780937)
XLA Ops:
  7.2 89.3 %while.12 = (s32[]{:T(128)}, f32[8,512,128]{2,1,0:T(8,128)}, s32[]{:T(128)}, s32[8]{0:T(128)S(1)}, s32[]{:T(128)}, /*index=5*/bf16[128,8192]{1,0:T(8,128)(2,1)}, s32[]{:T(128)}) while((s32[]{:T(128)}, f32[8,512,128]{2,1,0:T(8,128)}, s32[]{:T(128)}, s32[8]{0:T(128)S(1)}, s32[]{:T(128)}, /*index=5*/bf16[128,8192]{1,0:T(8,128)(2,1)}, ...), condition=%wide.region_1.2_spmd, body=%wide.region_0.1_spmd.sunk | while | flops 1128285184 | bytes 2430049 | solution.py:66
  7.2 0.6 dynamic_slice.8
  7.8 0.6 add_multiply_fusion.4
  8.4 9.9 %fusion.90 = f32[8,512,128]{2,1,0:T(8,128)} fusion(f32[8,512,128]{2,1,0:T(8,128)} %get-tuple-element.147, s32[]{:T(128)} %get-tuple-element.146, bf16[128,8192]{1,0:T(8,128)(2,1)} %get-tuple-element.158, s32[]{:T(128)} %get-tuple-element.157, s32[512]{0:T(512)S(1)} %add_multiply_fusion.4, s32[8192]{0:T(1024)S(1)} %add_multiply_fusion.5), kind=kOutput, calls=%fused_computation.11.clone.1 | convolution fusion | flops 1128267776 | bytes 2395136 | tf_op jit(solution)/shard_map/while/body/eval_jaxpr/dot_general | solution.py:63
  18.4 0.6 dynamic_slice.8
  18.9 0.6 add_multiply_fusion.4
  19.6 9.9 %fusion.90 = f32[8,512,128]{2,1,0:T(8,128)} fusion(f32[8,512,128]{2,1,0:T(8,128)} %get-tuple-element.147, s32[]{:T(128)} %get-tuple-element.146, bf16[128,8192]{1,0:T(8,128)(2,1)} %get-tuple-element.158, s32[]{:T(128)} %get-tuple-element.157, s32[512]{0:T(512)S(1)} %add_multiply_fusion.4, s32[8192]{0:T(1024)S(1)} %add_multiply_fusion.5), kind=kOutput, calls=%fused_computation.11.clone.1 | convolution fusion | flops 1128267776 | bytes 2395136 | tf_op jit(solution)/shard_map/while/body/eval_jaxpr/dot_general | solution.py:63
  29.5 0.6 dynamic_slice.8
  30.1 0.6 add_multiply_fusion.4
  30.7 9.9 %fusion.90 = f32[8,512,128]{2,1,0:T(8,128)} fusion(f32[8,512,128]{2,1,0:T(8,128)} %get-tuple-element.147, s32[]{:T(128)} %get-tuple-element.146, bf16[128,8192]{1,0:T(8,128)(2,1)} %get-tuple-element.158, s32[]{:T(128)} %get-tuple-element.157, s32[512]{0:T(512)S(1)} %add_multiply_fusion.4, s32[8192]{0:T(1024)S(1)} %add_multiply_fusion.5), kind=kOutput, calls=%fused_computation.11.clone.1 | convolution fusion | flops 1128267776 | bytes 2395136 | tf_op jit(solution)/shard_map/while/body/eval_jaxpr/dot_general | solution.py:63
  40.7 0.6 dynamic_slice.8
  41.2 0.6 add_multiply_fusion.4
  41.9 9.9 %fusion.90 = f32[8,512,128]{2,1,0:T(8,128)} fusion(f32[8,512,128]{2,1,0:T(8,128)} %get-tuple-element.147, s32[]{:T(128)} %get-tuple-element.146, bf16[128,8192]{1,0:T(8,128)(2,1)} %get-tuple-element.158, s32[]{:T(128)} %get-tuple-element.157, s32[512]{0:T(512)S(1)} %add_multiply_fusion.4, s32[8192]{0:T(1024)S(1)} %add_multiply_fusion.5), kind=kOutput, calls=%fused_computation.11.clone.1 | convolution fusion | flops 1128267776 | bytes 2395136 | tf_op jit(solution)/shard_map/while/body/eval_jaxpr/dot_general | solution.py:63
  51.8 0.6 dynamic_slice.8
  52.4 0.6 add_multiply_fusion.4
  53.0 9.9 %fusion.90 = f32[8,512,128]{2,1,0:T(8,128)} fusion(f32[8,512,128]{2,1,0:T(8,128)} %get-tuple-element.147, s32[]{:T(128)} %get-tuple-element.146, bf16[128,8192]{1,0:T(8,128)(2,1)} %get-tuple-element.158, s32[]{:T(128)} %get-tuple-element.157, s32[512]{0:T(512)S(1)} %add_multiply_fusion.4, s32[8192]{0:T(1024)S(1)} %add_multiply_fusion.5), kind=kOutput, calls=%fused_computation.11.clone.1 | convolution fusion | flops 1128267776 | bytes 2395136 | tf_op jit(solution)/shard_map/while/body/eval_jaxpr/dot_general | solution.py:63
  63.0 0.6 dynamic_slice.8
  63.6 0.6 add_multiply_fusion.4
  64.2 9.9 %fusion.90 = f32[8,512,128]{2,1,0:T(8,128)} fusion(f32[8,512,128]{2,1,0:T(8,128)} %get-tuple-element.147, s32[]{:T(128)} %get-tuple-element.146, bf16[128,8192]{1,0:T(8,128)(2,1)} %get-tuple-element.158, s32[]{:T(128)} %get-tuple-element.157, s32[512]{0:T(512)S(1)} %add_multiply_fusion.4, s32[8192]{0:T(1024)S(1)} %add_multiply_fusion.5), kind=kOutput, calls=%fused_computation.11.clone.1 | convolution fusion | flops 1128267776 | bytes 2395136 | tf_op jit(solution)/shard_map/while/body/eval_jaxpr/dot_general | solution.py:63
  74.2 0.6 dynamic_slice.8
  74.7 0.6 add_multiply_fusion.4
  75.4 9.9 %fusion.90 = f32[8,512,128]{2,1,0:T(8,128)} fusion(f32[8,512,128]{2,1,0:T(8,128)} %get-tuple-element.147, s32[]{:T(128)} %get-tuple-element.146, bf16[128,8192]{1,0:T(8,128)(2,1)} %get-tuple-element.158, s32[]{:T(128)} %get-tuple-element.157, s32[512]{0:T(512)S(1)} %add_multiply_fusion.4, s32[8192]{0:T(1024)S(1)} %add_multiply_fusion.5), kind=kOutput, calls=%fused_computation.11.clone.1 | convolution fusion | flops 1128267776 | bytes 2395136 | tf_op jit(solution)/shard_map/while/body/eval_jaxpr/dot_general | solution.py:63
  85.3 0.6 dynamic_slice.8
  85.9 0.6 add_multiply_fusion.4
  86.5 9.9 %fusion.90 = f32[8,512,128]{2,1,0:T(8,128)} fusion(f32[8,512,128]{2,1,0:T(8,128)} %get-tuple-element.147, s32[]{:T(128)} %get-tuple-element.146, bf16[128,8192]{1,0:T(8,128)(2,1)} %get-tuple-element.158, s32[]{:T(128)} %get-tuple-element.157, s32[512]{0:T(512)S(1)} %add_multiply_fusion.4, s32[8192]{0:T(1024)S(1)} %add_multiply_fusion.5), kind=kOutput, calls=%fused_computation.11.clone.1 | convolution fusion | flops 1128267776 | bytes 2395136 | tf_op jit(solution)/shard_map/while/body/eval_jaxpr/dot_general | solution.py:63
  96.7 70.8 %reduce-scatter.2.cloned.1.call-done = f32[512,128]{1,0:T(8,128)} async-done(((f32[4096,128]{1,0:T(8,128)}), f32[512,128]{1,0:T(8,128)}) %reduce-scatter.2.cloned.1.call-update) | async-done | bytes 262160 | tf_op jit(solution)/shard_map/reduce_scatter | solution.py:67
  167.6 1.0 convert_element_type.31
  168.5 0.9 fusion.31
  169.5 31.4 %all-reduce.2.cloned.1.call-done = f32[4,128,128]{2,1,0:T(8,128)} async-done(((f32[4,128,128]{2,1,0:T(8,128)}), f32[4,128,128]{2,1,0:T(8,128)}) %all-reduce.2.cloned.1.call-update) | async-done | bytes 262160 | tf_op jit(solution)/shard_map/psum | solution.py:84
  200.9 1.1 select_reduce_fusion.1
  202.0 1.2 select_reduce_fusion
  203.1 0.4 convolution_subtract_fusion.9
  203.6 0.4 fusion.22
  204.0 0.4 convolution_subtract_fusion.8
  204.8 0.4 convolution_subtract_fusion.7
  205.6 0.4 convolution_subtract_fusion.6
  206.4 0.4 convolution_subtract_fusion.5
  207.2 0.4 convolution_subtract_fusion.4
  208.0 0.4 convolution_subtract_fusion.3
  208.9 0.4 convolution_subtract_fusion.2
  209.7 0.4 convolution_subtract_fusion.1
  210.9 0.6 convolution_convert_fusion
  211.9 12.6 %all_to_all.38 = bf16[512,8,16]{0,2,1:T(8,128)(2,1)S(1)} all-to-all(bf16[512,8,16]{0,2,1:T(8,128)(2,1)S(1)} %all_to_all.28), channel_id=1, replica_groups=mesh['param'=8,'ex'=4] {'param'}, dimensions={1} | all-to-all | bytes 262144 | tf_op jit(solution)/shard_map/all_to_all | solution.py:92
  224.5 3.4 %convolution_bitcast_fusion = f32[512,16]{0,1:T(8,128)S(1)} fusion(bf16[4096,16]{0,1:T(8,128)(2,1)S(1)} %bitcast.78, bf16[512,4096]{1,0:T(8,128)(2,1)} %param.7), kind=kOutput, calls=%fused_computation.33 | convolution fusion | flops 67108864 | bytes 4358144 | tf_op jit(solution)/shard_map/dot_general | solution.py:93
  228.1 9.1 %all_to_all.39 = f32[8,1,1024]{2,1,0:T(1,128)S(1)} all-to-all(f32[8,1,1024]{2,1,0:T(1,128)S(1)} %reshape.49), channel_id=1, replica_groups=mesh['param'=8,'ex'=4] {'param'}, dimensions={0} | all-to-all | bytes 65536 | tf_op jit(solution)/shard_map/all_to_all | solution.py:47
  237.2 0.5 broadcast.157
  237.7 0.7 reduce
  238.5 0.7 copy.8
  (34 shorter events, 4.6 us)
Async XLA Ops:
  6.5 161.0 %reduce-scatter.2.cloned.1.call-start = ((), (), s32[]{:S(2)}) async-start(), calls=%async_computation.3 | async-start | bytes 2359296 | tf_op jit(solution)/shard_map/reduce_scatter | solution.py:67
  96.5 104.4 %all-reduce.2.cloned.1.call-start = ((), (), s32[]{:S(2)}) async-start(), calls=%async_computation.4 | async-start | bytes 524288 | tf_op jit(solution)/shard_map/psum | solution.py:84
Sparse Core Ops, SparseCore 0:
  96.6 70.8 reduce-scatter.1
  169.9 30.9 all-reduce.1
where the time goes:
time: 247 us; the launch traced here: 246 us
  waiting for transfers between devices  102 us (41%)
  matrix products  92 us (37%)
  blocking collectives  21.7 us (9%)
  between operations  14.3 us (6%)
  other arithmetic  8.99 us (4%)
  local copies, waits for them, and re-layouts  6.42 us (3%)
    dot_general x8, matrix products, project_piece(): return jnp.dot(gradients, matrix, preferred_element_type=jnp.float32).T  79.4 us
    reduce_scatter x1, waiting for transfers between devices, on_device(): lax.psum_scatter(pieces.reshape(feats_owned * lax.axis_size('param'), exa...  70.8 us
    psum x1, waiting for transfers between devices, on_device(): fisher = lax.psum(partial_fisher, 'ex') / examples_total  31.4 us
    all_to_all x1, blocking collectives, on_device(): lax.all_to_all(conditioned, 'param', split_axis=1, concat_axis=0, tiled=T...  12.6 us
    all_to_all x1, blocking collectives, to_targets(): lax.all_to_all(partial_scores, 'param', split_axis=0, concat_axis=1, tile...  9.06 us
    mul x16, other arithmetic, hashed(): mixed = row_index * 73856093 ^ col_index * 19349663 ^ seed_value * 83492791  5.03 us
  transfers between devices with their start and end apart: 2, of which 2 were waited for; matrix products, arithmetic and copies ran while one was open for 0% of the time, Pallas kernels for 0%

commit v1 on v0

--- a/solution.py
+++ b/solution.py
@@ -1,16 +1,285 @@
+import functools
 import math
 
 import jax
 import jax.numpy as jnp
 from jax import lax
+from jax.experimental import pallas as pl
+from jax.experimental.pallas import tpu as pltpu
 from jax.sharding import PartitionSpec as P
 
 FEATS = 4096
 BLOCK = 128
 STEPS = 10
-
-
 DAMPING = 0.001
+MESH = pl.DeviceIdType.MESH
+
+
+def row_part(start, shape, seed_value):
+    row = start + lax.broadcasted_iota(jnp.int32, shape, 0)
+    mixed = row * 73856093 ^ seed_value * 83492791
+    return mixed ^ jnp.right_shift(mixed, 13) ^ jnp.int32(-(2**31))
+
+
+def col_part(start, shape):
+    col = start + lax.broadcasted_iota(jnp.int32, shape, 1)
+    mixed = col * 19349663
+    return mixed ^ jnp.right_shift(mixed, 13)
+
+
+def centred(rows, cols):
+    mixed = (rows ^ cols) * 1274126177
+    mixed = mixed ^ jnp.left_shift(mixed, 16)
+    return jnp.right_shift(mixed, 16).astype(jnp.float32).astype(jnp.bfloat16)
+
+
+def body(
+    sizes, seed_ref, grad_ref, target_ref, out_ref,
+    grads, rows_tab, cols_tab, tile_a, tile_b, targets, acc, mine, xs, xr, zs, zr, ys, feats,
+    pre, pre_all, part, part_bf, part_in,
+    local_sem, grad_sem, x_sem, z_sem, y_sem, pre_sem, score_sem,
+):
+    n_param, n_ex, exam_dev, coord_dev, target_rows, depth = sizes
+    n_far, n_y = n_param // 2, n_ex // 2
+    width = n_y * BLOCK
+    p, e = lax.axis_index("param"), lax.axis_index("ex")
+    z, x, y, c = p // 2, p % 2, e // 2, e % 2
+    pair = 2 * exam_dev
+    total_coords = coord_dev * n_param
+
+    def copy(src, dst, sem, slot, pp, ee):
+        return pltpu.make_async_remote_copy(
+            src_ref=src, dst_ref=dst, send_sem=sem.at[0, slot], recv_sem=sem.at[1, slot],
+            device_id=(pp, ee), device_id_type=MESH,
+        )
+
+    own_rows = pl.ds(pl.multiple_of(c * exam_dev, exam_dev), exam_dev)
+    load_grad = pltpu.make_async_copy(grad_ref, grads.at[own_rows], local_sem.at[0])
+    load_grad.start()
+    own_cols = pl.ds(pl.multiple_of(p * (n_ex * BLOCK), n_ex * BLOCK), n_ex * BLOCK)
+    load_target = pltpu.make_async_copy(target_ref.at[:, own_cols], targets, local_sem.at[1])
+    load_target.start()
+
+    barrier = pltpu.get_barrier_semaphore()
+    for d in range(1, n_param):
+        pl.semaphore_signal(barrier, inc=1, device_id=((p + d) % n_param, e), device_id_type=MESH)
+    for d in range(1, n_ex):
+        pl.semaphore_signal(barrier, inc=1, device_id=(p, (e + d) % n_ex), device_id_type=MESH)
+
+    seed_value = seed_ref[0]
+    rows_tab[...] = row_part(p * coord_dev, rows_tab.shape, seed_value)
+
+    order = [("x", 0)]
+    for s in range(1, n_far):
+        order += [("x", s), ("m", s - 1)]
+    order += [("m", n_far - 1)]
+
+    def far(s):
+        return (z + 1 + s) % n_far
+
+    for i, (kind, s) in enumerate(order):
+        to = far(s) * 2 + (1 - x if kind == "x" else x)
+        cols_tab[i] = col_part(to * (n_ex * BLOCK) + c * width, (8, width))
+    cols_tab[len(order)] = cols_tab[0]
+
+    tiles = coord_dev // depth
+
+    def make(tile, t, i):
+        start = pl.multiple_of(t * depth, depth)
+        cols = cols_tab[i]
+        for w in range(0, width, BLOCK):
+            col = cols[0:1, w : w + BLOCK]
+            tile[:, w : w + BLOCK] = centred(rows_tab[pl.ds(start, depth), :], col)
+
+    def use(tile, t):
+        start = pl.multiple_of(t * depth, depth)
+        acc[...] += jnp.dot(
+            grads[:, pl.ds(start, depth)], tile[...], preferred_element_type=jnp.float32
+        )
+
+    make(tile_a, 0, 0)
+    pl.semaphore_wait(barrier, n_param - 1 + n_ex - 1)
+    swap = copy(grad_ref, grads.at[own_rows], grad_sem, 0, p, e + 1 - 2 * c)
+    swap.start()
+    load_grad.wait()
+    swap.wait()
+
+    x_copies, z_copies = [], []
+    for i, (kind, s) in enumerate(order):
+        acc[...] = jnp.zeros_like(acc)
+
+        def step(t, carry):
+            make(tile_b, 2 * t + 1, i)
+            use(tile_a, 2 * t)
+            later = (2 * t + 2) // tiles
+            make(tile_a, 2 * t + 2 - later * tiles, i + later)
+            use(tile_b, 2 * t + 1)
+            return carry
+
+        lax.fori_loop(0, tiles // 2, step, 0)
+        if kind == "x":
+            xs[s] = acc[...].astype(jnp.bfloat16)
+            copy_x = copy(xs.at[s], xr.at[s], x_sem, s, p + 1 - 2 * x, e)
+            copy_x.start()
+            x_copies.append(copy_x)
+        else:
+            x_copies[s].wait_recv()
+            both = acc[...] + xr[s].astype(jnp.float32)
+            if s < n_far - 1:
+                zs[s] = both.astype(jnp.bfloat16)
+                copy_z = copy(zs.at[s], zr.at[s], z_sem, s, far(s) * 2 + x, e)
+                copy_z.start()
+                z_copies.append(copy_z)
+            else:
+                mine[...] = both
+
+    total = mine[...]
+    for s in range(n_far - 1):
+        z_copies[s].wait_recv()
+        total = total + zr[s].astype(jnp.float32)
+    total = (total * (math.sqrt(3.0 / total_coords) / 32768.0)).astype(jnp.bfloat16)
+    for k in range(n_y):
+        ys[k] = total[:, k * BLOCK : (k + 1) * BLOCK]
+    my_pair = pl.ds(pl.multiple_of(y * pair, pair), pair)
+    y_copies = []
+    for d in range(1, n_y):
+        there = (y + d) % n_y
+        copy_y = copy(ys.at[there], feats.at[my_pair], y_sem, d - 1, p, there * 2 + c)
+        copy_y.start()
+        y_copies.append(copy_y)
+    feats[my_pair, :] = ys[y]
+    for copy_y in y_copies:
+        copy_y.wait_recv()
+
+    fisher = lax.dot_general(
+        feats[...], feats[...], (((0,), (0,)), ((), ())), preferred_element_type=jnp.float32
+    ) / (n_ex * exam_dev)
+    eye = (
+        lax.broadcasted_iota(jnp.int32, (BLOCK, BLOCK), 0)
+        == lax.broadcasted_iota(jnp.int32, (BLOCK, BLOCK), 1)
+    ).astype(jnp.float32)
+
+    def trace(square):
+        return jnp.sum(jnp.sum(square * eye, axis=0, keepdims=True), axis=1, keepdims=True)
+
+    damped = fisher + (DAMPING * trace(fisher)) * eye
+    inverse = eye / trace(damped)
+    gap = eye - damped / trace(damped)
+    for step_index in range(STEPS):
+        if step_index < STEPS - 1:
+            both = jnp.dot(
+                jnp.concatenate([inverse, gap], 0), gap,
+                precision=lax.Precision.HIGHEST, preferred_element_type=jnp.float32,
+            )
+            inverse, gap = inverse + both[:BLOCK], both[BLOCK:]
+        else:
+            inverse = inverse + jnp.dot(
+                inverse, gap, precision=lax.Precision.HIGHEST, preferred_element_type=jnp.float32
+            )
+    pre[...] = jnp.dot(
+        feats[...], inverse.astype(jnp.bfloat16), preferred_element_type=jnp.float32
+    ).astype(jnp.bfloat16)
+
+    slot = pl.ds(pl.multiple_of((c * n_y + y) * BLOCK, BLOCK), BLOCK)
+    pre_copies = []
+    for d in range(1, n_ex):
+        there = (e + d) % n_ex
+        src = pre.at[pl.ds(pl.multiple_of(there * exam_dev, exam_dev), exam_dev)]
+        copy_p = copy(src, pre_all.at[:, slot], pre_sem, d - 1, p, there)
+        copy_p.start()
+        pre_copies.append(copy_p)
+    pre_all[:, slot] = pre[pl.ds(pl.multiple_of(e * exam_dev, exam_dev), exam_dev), :]
+    load_target.wait()
+    for copy_p in pre_copies:
+        copy_p.wait_recv()
+
+    part[...] = lax.dot_general(
+        targets[...], pre_all[...], (((1,), (1,)), ((), ())), preferred_element_type=jnp.float32
+    )
+    part_bf[...] = part[...].astype(jnp.bfloat16)
+    t_dev = target_rows // n_param
+    score_copies = []
+    for d in range(1, n_param):
+        there = (p + d) % n_param
+        src = part_bf.at[pl.ds(pl.multiple_of(there * t_dev, t_dev), t_dev)]
+        copy_s = copy(src, part_in.at[d - 1], score_sem, d - 1, there, e)
+        copy_s.start()
+        score_copies.append(copy_s)
+    result = part[pl.ds(pl.multiple_of(p * t_dev, t_dev), t_dev), :]
+    for d in range(1, n_param):
+        score_copies[d - 1].wait_recv()
+        result = result + part_in[d - 1].astype(jnp.float32)
+    out_ref[...] = result
+    for group in (x_copies, z_copies, y_copies, pre_copies, score_copies):
+        for one in group:
+            one.wait_send()
+
+
+def fused(gradients, projection_seed, target_features):
+    n_param, n_ex = lax.axis_size("param"), lax.axis_size("ex")
+    exam_dev, coord_dev = gradients.shape
+    target_rows = target_features.shape[0]
+    n_far, n_y = n_param // 2, n_ex // 2
+    width, pair = n_y * BLOCK, 2 * exam_dev
+    t_dev = target_rows // n_param
+    depth = math.gcd(coord_dev // 2, 1024)
+    bf, f32 = jnp.bfloat16, jnp.float32
+    sizes = (n_param, n_ex, exam_dev, coord_dev, target_rows, depth)
+    dma = pltpu.SemaphoreType.DMA
+    return pl.pallas_call(
+        functools.partial(body, sizes),
+        out_shape=jax.ShapeDtypeStruct((t_dev, exam_dev), f32),
+        in_specs=[
+            pl.BlockSpec(memory_space=pltpu.SMEM),
+            pl.BlockSpec(memory_space=pl.ANY),
+            pl.BlockSpec(memory_space=pl.ANY),
+        ],
+        out_specs=pl.BlockSpec(memory_space=pltpu.VMEM),
+        scratch_shapes=[
+            pltpu.VMEM((pair, coord_dev), bf),
+            pltpu.VMEM((coord_dev, BLOCK), jnp.int32),
+            pltpu.VMEM((n_param + 1, 8, width), jnp.int32),
+            pltpu.VMEM((depth, width), bf),
+            pltpu.VMEM((depth, width), bf),
+            pltpu.VMEM((target_rows, n_ex * BLOCK), bf),
+            pltpu.VMEM((pair, width), f32),
+            pltpu.VMEM((pair, width), f32),
+            pltpu.VMEM((n_far, pair, width), bf),
+            pltpu.VMEM((n_far, pair, width), bf),
+            pltpu.VMEM((n_far, pair, width), bf),
+            pltpu.VMEM((n_far, pair, width), bf),
+            pltpu.VMEM((n_y, pair, BLOCK), bf),
+            pltpu.VMEM((n_ex * exam_dev, BLOCK), bf),
+            pltpu.VMEM((n_ex * exam_dev, BLOCK), bf),
+            pltpu.VMEM((exam_dev, n_ex * BLOCK), bf),
+            pltpu.VMEM((target_rows, exam_dev), f32),
+            pltpu.VMEM((target_rows, exam_dev), bf),
+            pltpu.VMEM((n_param - 1, t_dev, exam_dev), bf),
+            dma((2,)),
+            dma((2, 1)),
+            dma((2, n_far)),
+            dma((2, n_far)),
+            dma((2, n_y)),
+            dma((2, n_ex)),
+            dma((2, n_param)),
+        ],
+        compiler_params=pltpu.CompilerParams(
+            collective_id=0, has_side_effects=True, vmem_limit_bytes=40 * 2**20
+        ),
+    )(projection_seed, gradients, target_features)
+
+
+def kernel_fits(gradients, target_features):
+    n_param, n_ex = lax.axis_size("param"), lax.axis_size("ex")
+    exam_dev, coord_dev = gradients.shape
+    return (
+        n_param * n_ex * BLOCK == FEATS
+        and n_param % 2 == 0
+        and n_ex % 2 == 0
+        and exam_dev % BLOCK == 0
+        and coord_dev % 2048 == 0
+        and target_features.shape[0] % (16 * n_param) == 0
+    )
 
 
 def partner_2(array, axis, distance):
@@ -48,6 +317,8 @@
 
 
 def on_device(gradients, projection_seed, target_features):
+    if kernel_fits(gradients, target_features):
+        return fused(gradients, projection_seed, target_features)
     seed_value = projection_seed[0]
     my_index = lax.axis_index("param")
     param_count = lax.axis_size("param")

time: 247 us -> 58.7 us (0.24)
  waiting for transfers between devices: 102 us -> 0 us
  matrix products: 92 us -> 0 us
  Pallas kernels: 0 us -> 53.5 us
  blocking collectives: 21.7 us -> 0 us
  between operations: 14.3 us -> 0.67 us
  other arithmetic: 8.99 us -> 0 us
    dot_general x31 -> x0, matrix products: 92 us -> none  [the longest x8 79.4 us: project_piece(): return jnp.dot(gradients, matrix, preferred_element_type=jnp.float32).T]
    reduce_scatter x1 -> x0, waiting for transfers between devices: 70.8 us -> none  [on_device(): lax.psum_scatter(pieces.reshape(feats_owned * lax.axis_size('param'), exa...]
    pallas_call x0 -> x1, Pallas kernels: none -> 53.5 us  [fused(): pl.pallas_call(functools.partial(body, sizes), out_shape=jax.ShapeDtypeSt...]
    psum x1 -> x0, waiting for transfers between devices: 31.4 us -> none  [on_device(): fisher = lax.psum(partial_fisher, 'ex') / examples_total]
    all_to_all x2 -> x0, blocking collectives: 21.7 us -> none  [the longest x1 12.6 us: on_device(): lax.all_to_all(conditioned, 'param', split_axis=1, concat_axis=0, tiled=T...]
    mul x19 -> x0, other arithmetic: 5.05 us -> none  [the longest x16 5.03 us: hashed(): mixed = row_index * 73856093 ^ col_index * 19349663 ^ seed_value * 83492791]
    dynamic_slice x8 -> x0, local copies, waits for them, and re-layouts: 4.72 us -> none  [on_device(): pieces = lax.map(project_piece, starts)]
    unnamed x2 -> x5, local copies, waits for them, and re-layouts: 0.18 us -> 4.39 us
  transfers between devices with their start and end apart: 2 -> 0, of which waited for: 2 -> 0; matrix products, arithmetic and copies ran while one was open for 0% -> 0% of each run, Pallas kernels for 0% -> 0%
where the time goes in v1:
time: 58.7 us; the launch traced here: 58.5 us
  Pallas kernels  53.5 us (91%)
  local copies, waits for them, and re-layouts  4.39 us (7%)
  between operations  0.67 us (1%)
    pallas_call x1, Pallas kernels, fused(): pl.pallas_call(functools.partial(body, sizes), out_shape=jax.ShapeDtypeSt...  53.5 us
    unnamed x5, local copies, waits for them, and re-layouts  4.39 us

profile of v1, /device:TPU:0, one launch (start us, length us, event | category | flops | bytes accessed | tf_op | source)
XLA Modules:
  0.0 58.5 jit_solution(9531328504240048171)
XLA Ops:
  0.7 0.0 copy-start
  0.7 2.2 %copy-done = bf16[512,4096]{1,0:T(8,128)(2,1)S(1)} copy-done((bf16[512,4096]{1,0:T(8,128)(2,1)S(1)}, bf16[512,4096]{1,0:T(8,128)(2,1)}, u32[]{:S(2)}) %copy-start) | copy-done | bytes 4194328
  2.8 0.0 copy-start.1
  2.8 1.6 %copy-done.1 = bf16[128,8192]{1,0:T(8,128)(2,1)S(1)} copy-done((bf16[128,8192]{1,0:T(8,128)(2,1)S(1)}, bf16[128,8192]{1,0:T(8,128)(2,1)}, u32[]{:S(2)}) %copy-start.1) | copy-done | bytes 2097176
  4.4 53.5 %shard_map.37 = f32[64,128]{1,0:T(8,128)S(1)} custom-call(s32[1]{0:T(128)S(6)} %copy.5.seed_ref, bf16[128,8192]{1,0:T(8,128)(2,1)S(1)} %copy-done.1, bf16[512,4096]{1,0:T(8,128)(2,1)S(1)} %copy-done), custom_call_target="tpu_custom_call" | custom-call | tf_op jit(solution)/shard_map/pallas_call | solution.py:229
  57.9 0.6 %copy.6 = f32[64,128]{1,0:T(8,128)} copy(f32[64,128]{1,0:T(8,128)S(1)} %shard_map.37) | data formatting | bytes 65536
Async XLA Ops:
  0.7 2.2 %copy-start = (bf16[512,4096]{1,0:T(8,128)(2,1)S(1)}, bf16[512,4096]{1,0:T(8,128)(2,1)}, u32[]{:S(2)}) copy-start(bf16[512,4096]{1,0:T(8,128)(2,1)} %target_ref.1) | copy-start | bytes 12582916
  2.8 1.6 %copy-start.1 = (bf16[128,8192]{1,0:T(8,128)(2,1)S(1)}, bf16[128,8192]{1,0:T(8,128)(2,1)}, u32[]{:S(2)}) copy-start(bf16[128,8192]{1,0:T(8,128)(2,1)} %grad_ref.1) | copy-start | bytes 6291460

commit v2 on v1

--- a/solution.py
+++ b/solution.py
@@ -12,6 +12,7 @@
 BLOCK = 128
 STEPS = 10
 DAMPING = 0.001
+PIECE = 64
 MESH = pl.DeviceIdType.MESH
 
 
@@ -30,12 +31,12 @@
 def centred(rows, cols):
     mixed = (rows ^ cols) * 1274126177
     mixed = mixed ^ jnp.left_shift(mixed, 16)
-    return jnp.right_shift(mixed, 16).astype(jnp.float32).astype(jnp.bfloat16)
+    return jnp.right_shift(mixed, 16).astype(jnp.float32)
 
 
 def body(
     sizes, seed_ref, grad_ref, target_ref, out_ref,
-    grads, rows_tab, cols_tab, tile_a, tile_b, targets, acc, mine, xs, xr, zs, zr, ys, feats,
+    grads, rows_tab, cols_tab, proj_a, proj_b, targets, acc, mine, xs, xr, zs, zr, ys, feats,
     pre, pre_all, part, part_bf, part_in,
     local_sem, grad_sem, x_sem, z_sem, y_sem, pre_sem, score_sem,
 ):
@@ -80,43 +81,54 @@
     for i, (kind, s) in enumerate(order):
         to = far(s) * 2 + (1 - x if kind == "x" else x)
         cols_tab[i] = col_part(to * (n_ex * BLOCK) + c * width, (8, width))
-    cols_tab[len(order)] = cols_tab[0]
 
     tiles = coord_dev // depth
-
-    def make(tile, t, i):
+    projs = (proj_a, proj_b)
+
+    def make(proj, t, i):
         start = pl.multiple_of(t * depth, depth)
-        cols = cols_tab[i]
-        for w in range(0, width, BLOCK):
-            col = cols[0:1, w : w + BLOCK]
-            tile[:, w : w + BLOCK] = centred(rows_tab[pl.ds(start, depth), :], col)
-
-    def use(tile, t):
-        start = pl.multiple_of(t * depth, depth)
-        acc[...] += jnp.dot(
-            grads[:, pl.ds(start, depth)], tile[...], preferred_element_type=jnp.float32
-        )
-
-    make(tile_a, 0, 0)
+        for k in range(0, depth, PIECE):
+            here = pl.ds(pl.multiple_of(start + k, PIECE), PIECE)
+            rows = rows_tab[here, :].reshape(PIECE // 8, 8, BLOCK)
+            for w in range(0, width, BLOCK):
+                values = centred(rows, cols_tab[i, :, w : w + BLOCK][None])
+                proj[here, w : w + BLOCK] = values.reshape(PIECE, BLOCK).astype(jnp.bfloat16)
+
+    def use(proj, t):
+        here = pl.ds(pl.multiple_of(t * depth, depth), depth)
+        acc[...] += jnp.dot(grads[:, here], proj[here, :], preferred_element_type=jnp.float32)
+
+    def swap(t):
+        here = pl.ds(pl.multiple_of(t * depth, depth), depth)
+        return copy(grad_ref.at[:, here], grads.at[own_rows, here], grad_sem, t, p, e + 1 - 2 * c)
+
     pl.semaphore_wait(barrier, n_param - 1 + n_ex - 1)
-    swap = copy(grad_ref, grads.at[own_rows], grad_sem, 0, p, e + 1 - 2 * c)
-    swap.start()
+
+    def first(t, carry):
+        swap(t).start()
+        return carry
+
+    def ahead(t, carry):
+        make(projs[0], t, 0)
+        return carry
+
+    lax.fori_loop(0, tiles, first, 0)
+    lax.fori_loop(0, tiles, ahead, 0)
     load_grad.wait()
-    swap.wait()
 
     x_copies, z_copies = [], []
     for i, (kind, s) in enumerate(order):
         acc[...] = jnp.zeros_like(acc)
 
         def step(t, carry):
-            make(tile_b, 2 * t + 1, i)
-            use(tile_a, 2 * t)
-            later = (2 * t + 2) // tiles
-            make(tile_a, 2 * t + 2 - later * tiles, i + later)
-            use(tile_b, 2 * t + 1)
+            if i == 0:
+                swap(t).wait()
+            if i + 1 < len(order):
+                make(projs[(i + 1) % 2], t, i + 1)
+            use(projs[i % 2], t)
             return carry
 
-        lax.fori_loop(0, tiles // 2, step, 0)
+        lax.fori_loop(0, tiles, step, 0)
         if kind == "x":
             xs[s] = acc[...].astype(jnp.bfloat16)
             copy_x = copy(xs.at[s], xr.at[s], x_sem, s, p + 1 - 2 * x, e)
@@ -222,7 +234,7 @@
     n_far, n_y = n_param // 2, n_ex // 2
     width, pair = n_y * BLOCK, 2 * exam_dev
     t_dev = target_rows // n_param
-    depth = math.gcd(coord_dev // 2, 1024)
+    depth = math.gcd(coord_dev, 1024)
     bf, f32 = jnp.bfloat16, jnp.float32
     sizes = (n_param, n_ex, exam_dev, coord_dev, target_rows, depth)
     dma = pltpu.SemaphoreType.DMA
@@ -238,9 +250,9 @@
         scratch_shapes=[
             pltpu.VMEM((pair, coord_dev), bf),
             pltpu.VMEM((coord_dev, BLOCK), jnp.int32),
-            pltpu.VMEM((n_param + 1, 8, width), jnp.int32),
-            pltpu.VMEM((depth, width), bf),
-            pltpu.VMEM((depth, width), bf),
+            pltpu.VMEM((n_param, 8, width), jnp.int32),
+            pltpu.VMEM((coord_dev, width), bf),
+            pltpu.VMEM((coord_dev, width), bf),
             pltpu.VMEM((target_rows, n_ex * BLOCK), bf),
             pltpu.VMEM((pair, width), f32),
             pltpu.VMEM((pair, width), f32),
@@ -256,7 +268,7 @@
             pltpu.VMEM((target_rows, exam_dev), bf),
             pltpu.VMEM((n_param - 1, t_dev, exam_dev), bf),
             dma((2,)),
-            dma((2, 1)),
+            dma((2, coord_dev // depth)),
             dma((2, n_far)),
             dma((2, n_far)),
             dma((2, n_y)),
@@ -264,7 +276,7 @@
             dma((2, n_param)),
         ],
         compiler_params=pltpu.CompilerParams(
-            collective_id=0, has_side_effects=True, vmem_limit_bytes=40 * 2**20
+            collective_id=0, has_side_effects=True, vmem_limit_bytes=58 * 2**20
         ),
     )(projection_seed, gradients, target_features)
 

time: 58.7 us -> 59.3 us (1.010)
  Pallas kernels: 53.5 us -> 57.1 us
  local copies, waits for them, and re-layouts: 4.39 us -> 1.38 us
    pallas_call x1, Pallas kernels: 53.5 us -> 57.1 us  [fused(): pl.pallas_call(functools.partial(body, sizes), out_shape=jax.ShapeDtypeSt...]
    unnamed x5 -> x1, local copies, waits for them, and re-layouts: 4.39 us -> 1.38 us
where the time goes in v2:
time: 59.3 us; the launch traced here: 59.1 us
  Pallas kernels  57.1 us (96%)
  local copies, waits for them, and re-layouts  1.38 us (2%)
  between operations  0.66 us (1%)
    pallas_call x1, Pallas kernels, fused(): pl.pallas_call(functools.partial(body, sizes), out_shape=jax.ShapeDtypeSt...  57.1 us
    unnamed x1, local copies, waits for them, and re-layouts  1.38 us

profile of v2, /device:TPU:0, one launch (start us, length us, event | category | flops | bytes accessed | tf_op | source)
XLA Modules:
  0.0 59.1 jit_solution(17703097439998551056)
XLA Ops:
  0.7 57.1 %shard_map.37 = f32[64,128]{1,0:T(8,128)} custom-call(s32[1]{0:T(128)S(6)} %copy.5.seed_ref, bf16[128,8192]{1,0:T(8,128)(2,1)} %grad_ref.1, bf16[512,4096]{1,0:T(8,128)(2,1)} %target_ref.1), custom_call_target="tpu_custom_call" | custom-call | tf_op jit(solution)/shard_map/pallas_call | solution.py:241
  57.7 1.4 %copy.6 = f32[64,128]{1,0:T(8,128)} copy(f32[64,128]{1,0:T(8,128)} %shard_map.37) | data formatting | bytes 65536

commit v3 on v2

--- a/solution.py
+++ b/solution.py
@@ -67,23 +67,14 @@
     for d in range(1, n_ex):
         pl.semaphore_signal(barrier, inc=1, device_id=(p, (e + d) % n_ex), device_id_type=MESH)
 
-    seed_value = seed_ref[0]
-    rows_tab[...] = row_part(p * coord_dev, rows_tab.shape, seed_value)
-
-    order = [("x", 0)]
-    for s in range(1, n_far):
-        order += [("x", s), ("m", s - 1)]
-    order += [("m", n_far - 1)]
+    tiles = coord_dev // depth
+    projs = (proj_a, proj_b)
+
+    order = [("x", s) for s in range(n_far - 1)] + [("m", s) for s in range(n_far - 1)]
+    order += [("x", n_far - 1), ("m", n_far - 1)]
 
     def far(s):
         return (z + 1 + s) % n_far
-
-    for i, (kind, s) in enumerate(order):
-        to = far(s) * 2 + (1 - x if kind == "x" else x)
-        cols_tab[i] = col_part(to * (n_ex * BLOCK) + c * width, (8, width))
-
-    tiles = coord_dev // depth
-    projs = (proj_a, proj_b)
 
     def make(proj, t, i):
         start = pl.multiple_of(t * depth, depth)
@@ -102,8 +93,6 @@
         here = pl.ds(pl.multiple_of(t * depth, depth), depth)
         return copy(grad_ref.at[:, here], grads.at[own_rows, here], grad_sem, t, p, e + 1 - 2 * c)
 
-    pl.semaphore_wait(barrier, n_param - 1 + n_ex - 1)
-
     def first(t, carry):
         swap(t).start()
         return carry
@@ -112,7 +101,14 @@
         make(projs[0], t, 0)
         return carry
 
+    pl.semaphore_wait(barrier, n_param - 1 + n_ex - 1)
     lax.fori_loop(0, tiles, first, 0)
+    seed_value = seed_ref[0]
+    rows_tab[...] = row_part(p * coord_dev, rows_tab.shape, seed_value)
+    for i, (kind, s) in enumerate(order):
+        to = far(s) * 2 + (1 - x if kind == "x" else x)
+        cols_tab[i] = col_part(to * (n_ex * BLOCK) + c * width, (8, width))
+
     lax.fori_loop(0, tiles, ahead, 0)
     load_grad.wait()
 
@@ -234,7 +230,7 @@
     n_far, n_y = n_param // 2, n_ex // 2
     width, pair = n_y * BLOCK, 2 * exam_dev
     t_dev = target_rows // n_param
-    depth = math.gcd(coord_dev, 1024)
+    depth = math.gcd(coord_dev, 2048)
     bf, f32 = jnp.bfloat16, jnp.float32
     sizes = (n_param, n_ex, exam_dev, coord_dev, target_rows, depth)
     dma = pltpu.SemaphoreType.DMA

time: 59.3 us -> 55.5 us (0.936)
  Pallas kernels: 57.1 us -> 53.3 us
    pallas_call x1, Pallas kernels: 57.1 us -> 53.3 us  [fused(): pl.pallas_call(functools.partial(body, sizes), out_shape=jax.ShapeDtypeSt...]
where the time goes in v3:
time: 55.5 us; the launch traced here: 55.3 us
  Pallas kernels  53.3 us (96%)
  local copies, waits for them, and re-layouts  1.38 us (2%)
  between operations  0.66 us (1%)
    pallas_call x1, Pallas kernels, fused(): pl.pallas_call(functools.partial(body, sizes), out_shape=jax.ShapeDtypeSt...  53.3 us
    unnamed x1, local copies, waits for them, and re-layouts  1.38 us

profile of v3, /device:TPU:0, one launch (start us, length us, event | category | flops | bytes accessed | tf_op | source)
XLA Modules:
  0.0 55.3 jit_solution(10156884326338820986)
XLA Ops:
  0.7 53.3 %shard_map.37 = f32[64,128]{1,0:T(8,128)} custom-call(s32[1]{0:T(128)S(6)} %copy.5.seed_ref, bf16[128,8192]{1,0:T(8,128)(2,1)} %grad_ref.1, bf16[512,4096]{1,0:T(8,128)(2,1)} %target_ref.1), custom_call_target="tpu_custom_call" | custom-call | tf_op jit(solution)/shard_map/pallas_call | solution.py:237
  53.9 1.4 %copy.6 = f32[64,128]{1,0:T(8,128)} copy(f32[64,128]{1,0:T(8,128)} %shard_map.37) | data formatting | bytes 65536

commit v4 on v3

--- a/solution.py
+++ b/solution.py
@@ -68,10 +68,6 @@
         pl.semaphore_signal(barrier, inc=1, device_id=(p, (e + d) % n_ex), device_id_type=MESH)
 
     tiles = coord_dev // depth
-    projs = (proj_a, proj_b)
-
-    order = [("x", s) for s in range(n_far - 1)] + [("m", s) for s in range(n_far - 1)]
-    order += [("x", n_far - 1), ("m", n_far - 1)]
 
     def far(s):
         return (z + 1 + s) % n_far
@@ -98,52 +94,70 @@
         return carry
 
     def ahead(t, carry):
-        make(projs[0], t, 0)
+        make(proj_a, t, 0)
         return carry
 
     pl.semaphore_wait(barrier, n_param - 1 + n_ex - 1)
     lax.fori_loop(0, tiles, first, 0)
     seed_value = seed_ref[0]
     rows_tab[...] = row_part(p * coord_dev, rows_tab.shape, seed_value)
-    for i, (kind, s) in enumerate(order):
-        to = far(s) * 2 + (1 - x if kind == "x" else x)
+    for i in range(n_param):
+        to = far(i // 2) * 2 + (x if i % 2 else 1 - x)
         cols_tab[i] = col_part(to * (n_ex * BLOCK) + c * width, (8, width))
-
     lax.fori_loop(0, tiles, ahead, 0)
     load_grad.wait()
 
-    x_copies, z_copies = [], []
-    for i, (kind, s) in enumerate(order):
+    def run(i, now, later):
         acc[...] = jnp.zeros_like(acc)
 
         def step(t, carry):
-            if i == 0:
+            @pl.when(i == 0)
+            def _():
                 swap(t).wait()
-            if i + 1 < len(order):
-                make(projs[(i + 1) % 2], t, i + 1)
-            use(projs[i % 2], t)
+
+            if later is not None:
+                make(later, t, i + 1)
+            use(now, t)
             return carry
 
         lax.fori_loop(0, tiles, step, 0)
-        if kind == "x":
-            xs[s] = acc[...].astype(jnp.bfloat16)
-            copy_x = copy(xs.at[s], xr.at[s], x_sem, s, p + 1 - 2 * x, e)
-            copy_x.start()
-            x_copies.append(copy_x)
-        else:
-            x_copies[s].wait_recv()
-            both = acc[...] + xr[s].astype(jnp.float32)
-            if s < n_far - 1:
-                zs[s] = both.astype(jnp.bfloat16)
-                copy_z = copy(zs.at[s], zr.at[s], z_sem, s, far(s) * 2 + x, e)
-                copy_z.start()
-                z_copies.append(copy_z)
-            else:
-                mine[...] = both
-
-    total = mine[...]
+
+    def x_copy(s):
+        return copy(xs.at[s], xr.at[s], x_sem, s, p + 1 - 2 * x, e)
+
+    def z_copy(s):
+        return copy(zs.at[s], zr.at[s], z_sem, s, far(s) * 2 + x, e)
+
+    def send_x(s):
+        xs[s] = acc[...].astype(jnp.bfloat16)
+        x_copy(s).start()
+
+    def send_z(s):
+        x_copy(s).wait_recv()
+        zs[s] = (mine[...] + xr[s].astype(jnp.float32)).astype(jnp.bfloat16)
+        z_copy(s).start()
+
+    def both_chunks(s, carry):
+        run(2 * s, proj_a, proj_b)
+        send_x(s)
+
+        @pl.when(s > 0)
+        def _():
+            send_z(s - 1)
+
+        run(2 * s + 1, proj_b, proj_a)
+        mine[...] = acc[...]
+        return carry
+
+    lax.fori_loop(0, n_far - 1, both_chunks, 0)
+    run(n_param - 2, proj_a, proj_b)
+    send_x(n_far - 1)
+    send_z(n_far - 2)
+    run(n_param - 1, proj_b, None)
+    x_copy(n_far - 1).wait_recv()
+    total = acc[...] + xr[n_far - 1].astype(jnp.float32)
     for s in range(n_far - 1):
-        z_copies[s].wait_recv()
+        z_copy(s).wait_recv()
         total = total + zr[s].astype(jnp.float32)
     total = (total * (math.sqrt(3.0 / total_coords) / 32768.0)).astype(jnp.bfloat16)
     for k in range(n_y):
@@ -218,9 +232,9 @@
         score_copies[d - 1].wait_recv()
         result = result + part_in[d - 1].astype(jnp.float32)
     out_ref[...] = result
-    for group in (x_copies, z_copies, y_copies, pre_copies, score_copies):
-        for one in group:
-            one.wait_send()
+    sent = [x_copy(s) for s in range(n_far)] + [z_copy(s) for s in range(n_far - 1)]
+    for one in sent + y_copies + pre_copies + score_copies:
+        one.wait_send()
 
 
 def fused(gradients, projection_seed, target_features):
@@ -283,6 +297,7 @@
     return (
         n_param * n_ex * BLOCK == FEATS
         and n_param % 2 == 0
+        and n_param >= 4
         and n_ex % 2 == 0
         and exam_dev % BLOCK == 0
         and coord_dev % 2048 == 0

time: 55.5 us -> 56.3 us (1.014)
  Pallas kernels: 53.3 us -> 54 us
    pallas_call x1, Pallas kernels: 53.3 us -> 54 us  [fused(): pl.pallas_call(functools.partial(body, sizes), out_shape=jax.ShapeDtypeSt...]
where the time goes in v4:
time: 56.3 us; the launch traced here: 56.1 us
  Pallas kernels  54 us (96%)
  local copies, waits for them, and re-layouts  1.38 us (2%)
  between operations  0.66 us (1%)
    pallas_call x1, Pallas kernels, fused(): pl.pallas_call(functools.partial(body, sizes), out_shape=jax.ShapeDtypeSt...  54 us
    unnamed x1, local copies, waits for them, and re-layouts  1.38 us

profile of v4, /device:TPU:0, one launch (start us, length us, event | category | flops | bytes accessed | tf_op | source)
XLA Modules:
  0.0 56.1 jit_solution(10737727688585098642)
XLA Ops:
  0.7 54.0 %shard_map.37 = f32[64,128]{1,0:T(8,128)} custom-call(s32[1]{0:T(128)S(6)} %copy.5.seed_ref, bf16[128,8192]{1,0:T(8,128)(2,1)} %grad_ref.1, bf16[512,4096]{1,0:T(8,128)(2,1)} %target_ref.1), custom_call_target="tpu_custom_call" | custom-call | tf_op jit(solution)/shard_map/pallas_call | solution.py:251
  54.7 1.4 %copy.6 = f32[64,128]{1,0:T(8,128)} copy(f32[64,128]{1,0:T(8,128)} %shard_map.37) | data formatting | bytes 65536

commit v5 on v3

--- a/solution.py
+++ b/solution.py
@@ -32,6 +32,11 @@
     mixed = (rows ^ cols) * 1274126177
     mixed = mixed ^ jnp.left_shift(mixed, 16)
     return jnp.right_shift(mixed, 16).astype(jnp.float32)
+
+
+def split(values):
+    high = values.astype(jnp.bfloat16)
+    return high, (values - high.astype(jnp.float32)).astype(jnp.bfloat16)
 
 
 def body(
@@ -174,16 +179,16 @@
     inverse = eye / trace(damped)
     gap = eye - damped / trace(damped)
     for step_index in range(STEPS):
-        if step_index < STEPS - 1:
-            both = jnp.dot(
-                jnp.concatenate([inverse, gap], 0), gap,
-                precision=lax.Precision.HIGHEST, preferred_element_type=jnp.float32,
-            )
-            inverse, gap = inverse + both[:BLOCK], both[BLOCK:]
-        else:
-            inverse = inverse + jnp.dot(
-                inverse, gap, precision=lax.Precision.HIGHEST, preferred_element_type=jnp.float32
-            )
+        last = step_index == STEPS - 1
+        high, low = split(inverse if last else jnp.concatenate([inverse, gap], 0))
+        gap_high, gap_low = split(gap) if last else (high[BLOCK:], low[BLOCK:])
+        both = jnp.dot(
+            jnp.concatenate([high, low, high], 1),
+            jnp.concatenate([gap_high, gap_high, gap_low], 0),
+            preferred_element_type=jnp.float32,
+        )
+        inverse = inverse + both[:BLOCK]
+        gap = both[BLOCK:]
     pre[...] = jnp.dot(
         feats[...], inverse.astype(jnp.bfloat16), preferred_element_type=jnp.float32
     ).astype(jnp.bfloat16)
@@ -230,7 +235,7 @@
     n_far, n_y = n_param // 2, n_ex // 2
     width, pair = n_y * BLOCK, 2 * exam_dev
     t_dev = target_rows // n_param
-    depth = math.gcd(coord_dev, 2048)
+    depth = math.gcd(coord_dev, 4096)
     bf, f32 = jnp.bfloat16, jnp.float32
     sizes = (n_param, n_ex, exam_dev, coord_dev, target_rows, depth)
     dma = pltpu.SemaphoreType.DMA

time: 55.5 us -> 53.2 us (0.959)
  Pallas kernels: 53.3 us -> 51 us
    pallas_call x1, Pallas kernels: 53.3 us -> 51 us  [fused(): pl.pallas_call(functools.partial(body, sizes), out_shape=jax.ShapeDtypeSt...]
where the time goes in v5:
time: 53.2 us; the launch traced here: 53 us
  Pallas kernels  51 us (96%)
  local copies, waits for them, and re-layouts  1.38 us (3%)
  between operations  0.66 us (1%)
    pallas_call x1, Pallas kernels, fused(): pl.pallas_call(functools.partial(body, sizes), out_shape=jax.ShapeDtypeSt...  51 us
    unnamed x1, local copies, waits for them, and re-layouts  1.38 us

profile of v5, /device:TPU:0, one launch (start us, length us, event | category | flops | bytes accessed | tf_op | source)
XLA Modules:
  0.0 53.0 jit_solution(138092317185981935)
XLA Ops:
  0.7 51.0 %shard_map.37 = f32[64,128]{1,0:T(8,128)} custom-call(s32[1]{0:T(128)S(6)} %copy.5.seed_ref, bf16[128,8192]{1,0:T(8,128)(2,1)} %grad_ref.1, bf16[512,4096]{1,0:T(8,128)(2,1)} %target_ref.1), custom_call_target="tpu_custom_call" | custom-call | tf_op jit(solution)/shard_map/pallas_call | solution.py:242
  51.6 1.4 %copy.6 = f32[64,128]{1,0:T(8,128)} copy(f32[64,128]{1,0:T(8,128)} %shard_map.37) | data formatting | bytes 65536

commit v6 on v5

--- a/solution.py
+++ b/solution.py
@@ -13,6 +13,7 @@
 STEPS = 10
 DAMPING = 0.001
 PIECE = 64
+PART = 1024
 MESH = pl.DeviceIdType.MESH
 
 
@@ -72,8 +73,6 @@
     for d in range(1, n_ex):
         pl.semaphore_signal(barrier, inc=1, device_id=(p, (e + d) % n_ex), device_id_type=MESH)
 
-    tiles = coord_dev // depth
-    projs = (proj_a, proj_b)
 
     order = [("x", s) for s in range(n_far - 1)] + [("m", s) for s in range(n_far - 1)]
     order += [("x", n_far - 1), ("m", n_far - 1)]
@@ -81,74 +80,87 @@
     def far(s):
         return (z + 1 + s) % n_far
 
-    def make(proj, t, i):
-        start = pl.multiple_of(t * depth, depth)
-        for k in range(0, depth, PIECE):
-            here = pl.ds(pl.multiple_of(start + k, PIECE), PIECE)
-            rows = rows_tab[here, :].reshape(PIECE // 8, 8, BLOCK)
+    def half(t, start, size):
+        return pl.ds(pl.multiple_of(t * depth + start, size), size)
+
+    def make(proj, t, i, start, size):
+        for k in range(start, start + size, PIECE):
+            rows = rows_tab[half(t, k, PIECE), :].reshape(PIECE // 8, 8, BLOCK)
             for w in range(0, width, BLOCK):
                 values = centred(rows, cols_tab[i, :, w : w + BLOCK][None])
-                proj[here, w : w + BLOCK] = values.reshape(PIECE, BLOCK).astype(jnp.bfloat16)
-
-    def use(proj, t):
-        here = pl.ds(pl.multiple_of(t * depth, depth), depth)
-        acc[...] += jnp.dot(grads[:, here], proj[here, :], preferred_element_type=jnp.float32)
+                values = values.reshape(PIECE, BLOCK).astype(jnp.bfloat16)
+                proj[k : k + PIECE, w : w + BLOCK] = values
+
+    def block(now, t, later=None, later_t=None, later_i=None):
+        size = min(PART, depth)
+        for start in range(0, depth, size):
+            product = jnp.dot(
+                grads[:, half(t, start, size)], now[start : start + size, :],
+                preferred_element_type=jnp.float32,
+            )
+            if t == 0 and start == 0:
+                acc[...] = product
+            else:
+                acc[...] += product
+            if later is not None:
+                make(later, later_t, later_i, start, size)
 
     def swap(t):
-        here = pl.ds(pl.multiple_of(t * depth, depth), depth)
+        here = pl.ds(t * depth, depth)
         return copy(grad_ref.at[:, here], grads.at[own_rows, here], grad_sem, t, p, e + 1 - 2 * c)
 
-    def first(t, carry):
+    pl.semaphore_wait(barrier, n_param - 1 + n_ex - 1)
+    for t in range(2):
         swap(t).start()
-        return carry
-
-    def ahead(t, carry):
-        make(projs[0], t, 0)
-        return carry
-
-    pl.semaphore_wait(barrier, n_param - 1 + n_ex - 1)
-    lax.fori_loop(0, tiles, first, 0)
     seed_value = seed_ref[0]
     rows_tab[...] = row_part(p * coord_dev, rows_tab.shape, seed_value)
     for i, (kind, s) in enumerate(order):
         to = far(s) * 2 + (1 - x if kind == "x" else x)
         cols_tab[i] = col_part(to * (n_ex * BLOCK) + c * width, (8, width))
 
-    lax.fori_loop(0, tiles, ahead, 0)
+    make(proj_a, 0, 0, 0, depth)
     load_grad.wait()
 
-    x_copies, z_copies = [], []
-    for i, (kind, s) in enumerate(order):
-        acc[...] = jnp.zeros_like(acc)
-
-        def step(t, carry):
-            if i == 0:
-                swap(t).wait()
-            if i + 1 < len(order):
-                make(projs[(i + 1) % 2], t, i + 1)
-            use(projs[i % 2], t)
-            return carry
-
-        lax.fori_loop(0, tiles, step, 0)
-        if kind == "x":
+    def x_copy(s):
+        return copy(xs.at[s], xr.at[s], x_sem, s, p + 1 - 2 * x, e)
+
+    def z_copy(s):
+        return copy(zs.at[s], zr.at[s], z_sem, s, far(s) * 2 + x, e)
+
+    def swapped(t, i):
+        @pl.when(i == 0)
+        def _():
+            swap(t).wait()
+
+    def chunk(i, carry):
+        swapped(0, i)
+        block(proj_a, 0, proj_b, 1, i)
+        swapped(1, i)
+        block(proj_b, 1, proj_a, 0, i + 1)
+        to_pair = jnp.logical_or(i < n_far - 1, i == n_param - 2)
+
+        @pl.when(to_pair)
+        def _():
+            s = jnp.minimum(i, n_far - 1)
             xs[s] = acc[...].astype(jnp.bfloat16)
-            copy_x = copy(xs.at[s], xr.at[s], x_sem, s, p + 1 - 2 * x, e)
-            copy_x.start()
-            x_copies.append(copy_x)
-        else:
-            x_copies[s].wait_recv()
-            both = acc[...] + xr[s].astype(jnp.float32)
-            if s < n_far - 1:
-                zs[s] = both.astype(jnp.bfloat16)
-                copy_z = copy(zs.at[s], zr.at[s], z_sem, s, far(s) * 2 + x, e)
-                copy_z.start()
-                z_copies.append(copy_z)
-            else:
-                mine[...] = both
-
-    total = mine[...]
+            x_copy(s).start()
+
+        @pl.when(jnp.logical_not(to_pair))
+        def _():
+            s = i - (n_far - 1)
+            x_copy(s).wait_recv()
+            zs[s] = (acc[...] + xr[s].astype(jnp.float32)).astype(jnp.bfloat16)
+            z_copy(s).start()
+
+        return carry
+
+    lax.fori_loop(0, n_param - 1, chunk, 0)
+    block(proj_a, 0, proj_b, 1, n_param - 1)
+    block(proj_b, 1)
+    x_copy(n_far - 1).wait_recv()
+    total = acc[...] + xr[n_far - 1].astype(jnp.float32)
     for s in range(n_far - 1):
-        z_copies[s].wait_recv()
+        z_copy(s).wait_recv()
         total = total + zr[s].astype(jnp.float32)
     total = (total * (math.sqrt(3.0 / total_coords) / 32768.0)).astype(jnp.bfloat16)
     for k in range(n_y):
@@ -223,9 +235,9 @@
         score_copies[d - 1].wait_recv()
         result = result + part_in[d - 1].astype(jnp.float32)
     out_ref[...] = result
-    for group in (x_copies, z_copies, y_copies, pre_copies, score_copies):
-        for one in group:
-            one.wait_send()
+    sent = [x_copy(s) for s in range(n_far)] + [z_copy(s) for s in range(n_far - 1)]
+    for one in sent + y_copies + pre_copies + score_copies:
+        one.wait_send()
 
 
 def fused(gradients, projection_seed, target_features):
@@ -235,7 +247,7 @@
     n_far, n_y = n_param // 2, n_ex // 2
     width, pair = n_y * BLOCK, 2 * exam_dev
     t_dev = target_rows // n_param
-    depth = math.gcd(coord_dev, 4096)
+    depth = coord_dev // 2
     bf, f32 = jnp.bfloat16, jnp.float32
     sizes = (n_param, n_ex, exam_dev, coord_dev, target_rows, depth)
     dma = pltpu.SemaphoreType.DMA
@@ -252,8 +264,8 @@
             pltpu.VMEM((pair, coord_dev), bf),
             pltpu.VMEM((coord_dev, BLOCK), jnp.int32),
             pltpu.VMEM((n_param, 8, width), jnp.int32),
-            pltpu.VMEM((coord_dev, width), bf),
-            pltpu.VMEM((coord_dev, width), bf),
+            pltpu.VMEM((depth, width), bf),
+            pltpu.VMEM((depth, width), bf),
             pltpu.VMEM((target_rows, n_ex * BLOCK), bf),
             pltpu.VMEM((pair, width), f32),
             pltpu.VMEM((pair, width), f32),
@@ -288,6 +300,7 @@
     return (
         n_param * n_ex * BLOCK == FEATS
         and n_param % 2 == 0
+        and n_param >= 4
         and n_ex % 2 == 0
         and exam_dev % BLOCK == 0
         and coord_dev % 2048 == 0

time: 53.2 us -> 60.5 us (1.14)
  Pallas kernels: 51 us -> 58.3 us
    pallas_call x1, Pallas kernels: 51 us -> 58.3 us  [fused(): pl.pallas_call(functools.partial(body, sizes), out_shape=jax.ShapeDtypeSt...]
where the time goes in v6:
time: 60.5 us; the launch traced here: 60.3 us
  Pallas kernels  58.3 us (96%)
  local copies, waits for them, and re-layouts  1.38 us (2%)
  between operations  0.66 us (1%)
    pallas_call x1, Pallas kernels, fused(): pl.pallas_call(functools.partial(body, sizes), out_shape=jax.ShapeDtypeSt...  58.3 us
    unnamed x1, local copies, waits for them, and re-layouts  1.38 us

profile of v6, /device:TPU:0, one launch (start us, length us, event | category | flops | bytes accessed | tf_op | source)
XLA Modules:
  0.0 60.3 jit_solution(11510770927552885530)
XLA Ops:
  0.7 58.3 %shard_map.37 = f32[64,128]{1,0:T(8,128)} custom-call(s32[1]{0:T(128)S(6)} %copy.5.seed_ref, bf16[128,8192]{1,0:T(8,128)(2,1)} %grad_ref.1, bf16[512,4096]{1,0:T(8,128)(2,1)} %target_ref.1), custom_call_target="tpu_custom_call" | custom-call | tf_op jit(solution)/shard_map/pallas_call | solution.py:254
  58.9 1.4 %copy.6 = f32[64,128]{1,0:T(8,128)} copy(f32[64,128]{1,0:T(8,128)} %shard_map.37) | data formatting | bytes 65536

commit v7 on v6

--- a/solution.py
+++ b/solution.py
@@ -13,7 +13,6 @@
 STEPS = 10
 DAMPING = 0.001
 PIECE = 64
-PART = 1024
 MESH = pl.DeviceIdType.MESH
 
 
@@ -73,7 +72,6 @@
     for d in range(1, n_ex):
         pl.semaphore_signal(barrier, inc=1, device_id=(p, (e + d) % n_ex), device_id_type=MESH)
 
-
     order = [("x", s) for s in range(n_far - 1)] + [("m", s) for s in range(n_far - 1)]
     order += [("x", n_far - 1), ("m", n_far - 1)]
 
@@ -92,18 +90,13 @@
                 proj[k : k + PIECE, w : w + BLOCK] = values
 
     def block(now, t, later=None, later_t=None, later_i=None):
-        size = min(PART, depth)
-        for start in range(0, depth, size):
-            product = jnp.dot(
-                grads[:, half(t, start, size)], now[start : start + size, :],
-                preferred_element_type=jnp.float32,
-            )
-            if t == 0 and start == 0:
-                acc[...] = product
-            else:
-                acc[...] += product
-            if later is not None:
-                make(later, later_t, later_i, start, size)
+        if later is not None:
+            make(later, later_t, later_i, 0, depth)
+        product = jnp.dot(grads[:, half(t, 0, depth)], now[...], preferred_element_type=jnp.float32)
+        if t == 0:
+            acc[...] = product
+        else:
+            acc[...] += product
 
     def swap(t):
         here = pl.ds(t * depth, depth)

time: 60.5 us -> 60.5 us (level)
  no operation moved by 1% of the time
where the time goes in v7:
time: 60.5 us; the launch traced here: 60.3 us
  Pallas kernels  58.3 us (96%)
  local copies, waits for them, and re-layouts  1.38 us (2%)
  between operations  0.66 us (1%)
    pallas_call x1, Pallas kernels, fused(): pl.pallas_call(functools.partial(body, sizes), out_shape=jax.ShapeDtypeSt...  58.3 us
    unnamed x1, local copies, waits for them, and re-layouts  1.38 us

profile of v7, /device:TPU:0, one launch (start us, length us, event | category | flops | bytes accessed | tf_op | source)
XLA Modules:
  0.0 60.3 jit_solution(11510770927552885530)
XLA Ops:
  0.7 58.3 %shard_map.37 = f32[64,128]{1,0:T(8,128)} custom-call(s32[1]{0:T(128)S(6)} %copy.5.seed_ref, bf16[128,8192]{1,0:T(8,128)(2,1)} %grad_ref.1, bf16[512,4096]{1,0:T(8,128)(2,1)} %target_ref.1), custom_call_target="tpu_custom_call" | custom-call | tf_op jit(solution)/shard_map/pallas_call | solution.py:247
  58.9 1.4 %copy.6 = f32[64,128]{1,0:T(8,128)} copy(f32[64,128]{1,0:T(8,128)} %shard_map.37) | data formatting | bytes 65536

commit v8 on v5

--- a/solution.py
+++ b/solution.py
@@ -104,6 +104,7 @@
 
     def ahead(t, carry):
         make(projs[0], t, 0)
+        make(projs[1], t, 1)
         return carry
 
     pl.semaphore_wait(barrier, n_param - 1 + n_ex - 1)
@@ -124,7 +125,7 @@
         def step(t, carry):
             if i == 0:
                 swap(t).wait()
-            if i + 1 < len(order):
+            if 0 < i < len(order) - 1:
                 make(projs[(i + 1) % 2], t, i + 1)
             use(projs[i % 2], t)
             return carry

time: 53.2 us -> 52.6 us (0.989)
  Pallas kernels: 51 us -> 50.4 us
    pallas_call x1, Pallas kernels: 51 us -> 50.4 us  [fused(): pl.pallas_call(functools.partial(body, sizes), out_shape=jax.ShapeDtypeSt...]
where the time goes in v8:
time: 52.6 us; the launch traced here: 52.4 us
  Pallas kernels  50.4 us (96%)
  local copies, waits for them, and re-layouts  1.38 us (3%)
  between operations  0.66 us (1%)
    pallas_call x1, Pallas kernels, fused(): pl.pallas_call(functools.partial(body, sizes), out_shape=jax.ShapeDtypeSt...  50.4 us
    unnamed x1, local copies, waits for them, and re-layouts  1.38 us

profile of v8, /device:TPU:0, one launch (start us, length us, event | category | flops | bytes accessed | tf_op | source)
XLA Modules:
  0.0 52.4 jit_solution(8267274574642098416)
XLA Ops:
  0.7 50.4 %shard_map.37 = f32[64,128]{1,0:T(8,128)} custom-call(s32[1]{0:T(128)S(6)} %copy.5.seed_ref, bf16[128,8192]{1,0:T(8,128)(2,1)} %grad_ref.1, bf16[512,4096]{1,0:T(8,128)(2,1)} %target_ref.1), custom_call_target="tpu_custom_call" | custom-call | tf_op jit(solution)/shard_map/pallas_call | solution.py:243
  51.1 1.4 %copy.6 = f32[64,128]{1,0:T(8,128)} copy(f32[64,128]{1,0:T(8,128)} %shard_map.37) | data formatting | bytes 65536
